TPU v7x, 256 devices: a whole 4x4x8 slice. The times are simulated.
256 devices in a mesh: prow: 16 (over z, core), pcol: 16 (over x, y).
Axes of the slice: x: 4, y: 4, z: 8, core: 2. Of those that a mesh axis runs over, the one named last changes fastest.
Arguments:
- leaf_source: bfloat16 [16, 16, 8, 256, 128], P('prow', 'pcol'), may hold values from -6 to 6
- band_source: bfloat16 [16, 256, 128], P('prow'), may hold values from -6 to 6
- strip_source: bfloat16 [16, 256, 128], P('pcol'), may hold values from -6 to 6
- summit_source: bfloat16 [256, 128], replicated, may hold values from -6 to 6
- leaf_inverse: bfloat16 [16, 16, 8, 256, 256], P('prow', 'pcol'), may hold values from -1 to 2
- band_inverse: bfloat16 [16, 256, 256], P('prow'), may hold values from -1 to 2
- strip_inverse: bfloat16 [16, 256, 256], P('pcol'), may hold values from -1 to 2
- summit_inverse: bfloat16 [256, 256], replicated, may hold values from -1 to 2
- leaf_blocks: bfloat16 [16, 16, 28, 256, 256], P('prow', 'pcol'), may hold values from -0.09375 to 0.09375
- band_blocks: bfloat16 [16, 16, 8, 256, 256], P('prow', 'pcol'), may hold values from -0.0234375 to 0.0234375
- strip_blocks: bfloat16 [16, 16, 8, 256, 256], P('prow', 'pcol'), may hold values from -0.0234375 to 0.0234375
- summit_blocks: bfloat16 [16, 16, 8, 256, 256], P('prow', 'pcol'), may hold values from -0.015625 to 0.015625
- coupling: bfloat16 [16, 16, 256, 256], P('prow', 'pcol'), may hold values from -0.0625 to 0.0625
- summit_band: bfloat16 [16, 256, 256], P('prow', 'pcol'), may hold values from -0.046875 to 0.046875
- summit_strip: bfloat16 [16, 256, 256], P('pcol'), may hold values from -0.046875 to 0.046875
- parents: int32 [16, 16, 8], P('prow', 'pcol'), may hold values from 1 to 8, as said below
- widths: int32 [16, 16, 8], P('prow', 'pcol'), may hold values from 64 to 256
Outputs:
- leaf_answer: bfloat16 [16, 16, 8, 256, 128], P('prow', 'pcol')
- band_answer: bfloat16 [16, 256, 128], P('prow')
- strip_answer: bfloat16 [16, 256, 128], P('pcol')
- summit_answer: bfloat16 [256, 128], replicated
Inputs may be any that keep to these rules, and one draw needn't show every extreme that they name: parents[r, c, a] is a later leaf of the same subtree, or 8 where leaf a links only to the separators.
All inputs are finite; a program needn't handle non-finite values.
Results may differ from a plain program's by a relative error of at most 0.015.
Values sent between devices are 32-bit elements; how exact they have to be, the bound alone decides.
A program may use at most 64 MiB of HBM per device.

v0:
```python
import jax
import jax.numpy as jnp
from jax import lax
from jax.sharding import PartitionSpec as P

PASSES = 2


def ancestors(parent_list, leaf_count):
    node_ids = jnp.arange(leaf_count + 1, dtype=jnp.int32)
    current = parent_list
    extended = jnp.concatenate([current, jnp.full((1,), leaf_count, jnp.int32)])
    reached = jnp.zeros((leaf_count + 1, leaf_count), jnp.float32)
    for repeat in range(leaf_count):
        matches = current[None, :] == node_ids[:, None]
        reached = jnp.maximum(reached, matches.astype(jnp.float32))
        current = jnp.sum(jnp.where(matches, extended[:, None], 0), axis=0)
    return reached[:leaf_count]


def multiply(left, right, form):
    return jnp.einsum(form, left, right, preferred_element_type=jnp.float32)


def forward_block(inverse, source, partial_value):
    residual = (source.astype(jnp.float32) - partial_value).astype(jnp.bfloat16)
    return multiply(inverse, residual, "ij,jr->ir").astype(jnp.bfloat16)


def backward_block(inverse, source, partial_value):
    residual = (source.astype(jnp.float32) - partial_value).astype(jnp.bfloat16)
    return multiply(inverse, residual, "ji,jr->ir").astype(jnp.bfloat16)


def leaf_forward(pair_blocks, inverses, sources, reached, row_mask):
    leaf_count = sources.shape[0]
    solved = []
    for position in range(leaf_count):
        residual = sources[position].astype(jnp.float32)
        if position > 0:
            first_pair = position * (position - 1) // 2
            weights = reached[position, :position].astype(jnp.bfloat16)
            stacked = jnp.stack(solved) * weights[:, None, None]
            residual = residual - multiply(
                pair_blocks[first_pair : first_pair + position], stacked, "bij,bjr->ir"
            )
        residual = (row_mask[position] * residual).astype(jnp.bfloat16)
        solved.append(
            (row_mask[position] * multiply(inverses[position], residual, "ij,jr->ir")).astype(
                jnp.bfloat16
            )
        )
    return jnp.stack(solved)


def leaf_backward(pair_blocks, inverses, solved, outer, reached, row_mask):
    leaf_count = solved.shape[0]
    pending = outer
    answers = [None] * leaf_count
    for position in reversed(range(leaf_count)):
        residual = (
            row_mask[position] * (solved[position].astype(jnp.float32) - pending[position])
        ).astype(jnp.bfloat16)
        update = (row_mask[position] * multiply(inverses[position], residual, "ji,jr->ir")).astype(
            jnp.bfloat16
        )
        answers[position] = update
        if position > 0:
            first_pair = position * (position - 1) // 2
            pushed = multiply(
                pair_blocks[first_pair : first_pair + position], update, "bji,jr->bir"
            )
            pending = pending.at[:position].add(
                reached[position, :position][:, None, None] * pushed
            )
    return jnp.stack(answers)


def per_device(
    leaf_source,
    band_source,
    strip_source,
    summit_source,
    leaf_inverse,
    band_inverse,
    strip_inverse,
    summit_inverse,
    leaf_blocks,
    band_blocks,
    strip_blocks,
    summit_blocks,
    coupling,
    summit_band,
    summit_strip,
    parents,
    widths,
):
    leaf_count = leaf_source.shape[2]
    block_width = leaf_source.shape[3]
    reached = ancestors(parents[0, 0], leaf_count)
    column_ids = jnp.arange(block_width, dtype=jnp.int32)
    row_mask = (column_ids[None, :] < widths[0, 0][:, None]).astype(jnp.float32)[:, :, None]
    band_slab = summit_band.shape[1]
    strip_slab = block_width // lax.axis_size("prow")
    column_place = lax.axis_index("pcol") * band_slab
    row_place = lax.axis_index("prow") * strip_slab
    inverses = leaf_inverse[0, 0]
    pair_blocks = leaf_blocks[0, 0]
    to_band = band_blocks[0, 0]
    to_strip = strip_blocks[0, 0]
    to_summit = summit_blocks[0, 0]
    link_block = coupling[0, 0]
    lift_band = summit_band[0]
    lift_strip = summit_strip[0]
    current = (leaf_source[0, 0], band_source[0], strip_source[0], summit_source)
    for iteration in range(PASSES):
        leaf_now, band_now, strip_now, summit_now = current
        solved = leaf_forward(pair_blocks, inverses, leaf_now, reached, row_mask)
        band_term = multiply(to_band, solved, "aij,ajr->ir")
        strip_term = multiply(to_strip, solved, "aij,ajr->ir")
        summit_term = multiply(to_summit, solved, "aij,ajr->ir")
        band_partial = lax.psum(band_term, "pcol")
        band_solved = forward_block(band_inverse[0], band_now, band_partial)
        own_band = lax.dynamic_slice_in_dim(band_solved, column_place, band_slab, 0)
        summit_term = summit_term + multiply(lift_band, own_band, "ki,kn->in")
        strip_term = strip_term + multiply(link_block, band_solved, "ij,jn->in")
        strip_partial = lax.psum(strip_term, "prow")
        strip_solved = forward_block(strip_inverse[0], strip_now, strip_partial)
        own_lift = lax.dynamic_slice_in_dim(lift_strip, row_place, strip_slab, 0)
        own_strip = lax.dynamic_slice_in_dim(strip_solved, row_place, strip_slab, 0)
        summit_partial = lax.psum(
            summit_term + multiply(own_lift, own_strip, "ki,kn->in"), ("prow", "pcol")
        )
        summit_solved = forward_block(summit_inverse, summit_now, summit_partial)
        summit_answer = backward_block(
            summit_inverse, summit_solved, jnp.zeros(summit_solved.shape, jnp.float32)
        )
        strip_answer = backward_block(
            strip_inverse[0], strip_solved, multiply(lift_strip, summit_answer, "ki,in->kn")
        )
        downward = multiply(link_block, strip_answer, "ji,jn->in")
        band_piece = multiply(lift_band, summit_answer, "ki,in->kn")
        band_back = lax.psum(downward, "pcol") + lax.all_gather(
            band_piece, "pcol", axis=0, tiled=True
        )
        band_answer = backward_block(band_inverse[0], band_solved, band_back)
        outer = (
            multiply(to_band, band_answer, "aij,ir->ajr")
            + multiply(to_strip, strip_answer, "aij,ir->ajr")
            + multiply(to_summit, summit_answer, "aij,ir->ajr")
        )
        leaf_answer = leaf_backward(pair_blocks, inverses, solved, outer, reached, row_mask)
        current = (leaf_answer, band_answer, strip_answer, summit_answer)
    return (current[0][None, None], current[1][None], current[2][None], current[3])


def solution(mesh):
    placed = (
        P("prow", "pcol", None, None, None),
        P("prow", None, None),
        P("pcol", None, None),
        P(),
        P("prow", "pcol", None, None, None),
        P("prow", None, None),
        P("pcol", None, None),
        P(),
        P("prow", "pcol", None, None, None),
        P("prow", "pcol", None, None, None),
        P("prow", "pcol", None, None, None),
        P("prow", "pcol", None, None, None),
        P("prow", "pcol", None, None),
        P("prow", "pcol", None),
        P("pcol", None, None),
        P("prow", "pcol", None),
        P("prow", "pcol", None),
    )
    return jax.shard_map(
        per_device,
        mesh=mesh,
        in_specs=placed,
        out_specs=(
            P("prow", "pcol", None, None, None),
            P("prow", None, None),
            P("pcol", None, None),
            P(),
        ),
        check_vma=False,
    )
```

profile of v0, /device:TPU:2, one launch (start us, length us, event | category | flops | bytes accessed | tf_op | source)
XLA Modules:
  0.0 1181.8 jit_solution(3843605746356094015)
XLA Ops:
  14.1 1.9 constant_dynamic-update-slice_fusion.17
  15.9 2.0 constant_dynamic-update-slice_fusion.16
  17.9 2.1 constant_dynamic-update-slice_fusion.15
  20.0 2.1 constant_dynamic-update-slice_fusion.14
  22.1 2.2 constant_dynamic-update-slice_fusion.13
  25.3 2.5 constant_dynamic-update-slice_fusion.12
  28.6 2.6 constant_dynamic-update-slice_fusion.11
  31.2 2.6 constant_dynamic-update-slice_fusion.18
  33.8 2.2 convolution_bitcast_fusion.19
  42.3 2.1 convolution_bitcast_fusion.17
  44.4 2.1 convolution_bitcast_fusion.18
  46.5 84.6 %all-reduce.9.cloned.1.call-done = f32[256,128]{1,0:T(8,128)} async-done(((f32[256,128]{1,0:T(8,128)}), f32[256,128]{1,0:T(8,128)}) %all-reduce.9.cloned.1.call-update) | async-done | bytes 131088 | tf_op jit(solution)/shard_map/psum | solution.py:122
  133.0 1.7 fusion.29
  134.8 1.8 fusion.34
  136.7 105.3 %all-reduce.11.cloned.1.call-done = f32[256,128]{1,0:T(8,128)} async-done(((f32[256,128]{1,0:T(8,128)}), f32[256,128]{1,0:T(8,128)}) %all-reduce.11.cloned.1.call-update) | async-done | bytes 131088 | tf_op jit(solution)/shard_map/psum | solution.py:127
  243.8 1.8 convolution_add_fusion.8
  246.8 243.6 %all-reduce.13.cloned.1.call-done = f32[256,128]{1,0:T(8,128)} async-done(((f32[256,128]{1,0:T(8,128)}), f32[256,128]{1,0:T(8,128)}) %all-reduce.13.cloned.1.call-update) | async-done | bytes 131088 | tf_op jit(solution)/shard_map/psum | solution.py:131
  490.5 1.9 convolution_convert_fusion.8
  492.3 1.9 convolution_convert_fusion.7
  494.2 1.7 convolution_bitcast_fusion.10
  496.9 23.8 %all_gather.6 = f32[256,128]{1,0:T(8,128)} all-gather(f32[16,128]{1,0:T(8,128)S(1)} %convolution_bitcast_fusion.22), channel_id=1, replica_groups=mesh['prow'=16,'pcol'=16] {'pcol'}, dimensions={0}, use_global_device_ids=true | all-gather | bytes 139264 | tf_op jit(solution)/shard_map/all_gather | solution.py:143
  520.7 1.6 copy.39
  522.3 62.3 %all-reduce.15.cloned.1.call-done = f32[256,128]{0,1:T(8,128)} async-done(((f32[256,128]{0,1:T(8,128)}), f32[256,128]{0,1:T(8,128)}) %all-reduce.15.cloned.1.call-update) | async-done | bytes 131088 | tf_op jit(solution)/shard_map/psum | solution.py:143
  593.4 1.5 fusion.77
  594.9 2.0 constant_dynamic-update-slice_fusion.43
  596.9 2.1 constant_dynamic-update-slice_fusion.42
  599.0 2.2 constant_dynamic-update-slice_fusion.41
  601.2 2.4 constant_dynamic-update-slice_fusion.40
  603.6 2.4 constant_dynamic-update-slice_fusion.39
  606.0 2.5 constant_dynamic-update-slice_fusion.38
  608.5 2.6 constant_dynamic-update-slice_fusion.37
  611.1 2.7 constant_dynamic-update-slice_fusion.44
  613.8 2.2 convolution_bitcast_fusion.13
  616.0 2.2 convolution_bitcast_fusion.15
  618.2 2.2 convolution_bitcast_fusion.14
  620.4 89.7 %all-reduce.17.cloned.1.call-done = f32[256,128]{0,1:T(8,128)} async-done(((f32[256,128]{0,1:T(8,128)}), f32[256,128]{0,1:T(8,128)}) %all-reduce.17.cloned.1.call-update) | async-done | bytes 131088 | tf_op jit(solution)/shard_map/psum | solution.py:122
  712.0 1.8 fusion.27
  713.8 1.8 fusion.33
  715.6 105.4 %all-reduce.19.cloned.1.call-done = f32[256,128]{0,1:T(8,128)} async-done(((f32[256,128]{0,1:T(8,128)}), f32[256,128]{0,1:T(8,128)}) %all-reduce.19.cloned.1.call-update) | async-done | bytes 131088 | tf_op jit(solution)/shard_map/psum | solution.py:127
  822.8 1.8 convolution_add_fusion.6
  824.6 245.8 %all-reduce.21.cloned.1.call-done = f32[256,128]{0,1:T(8,128)} async-done(((f32[256,128]{0,1:T(8,128)}), f32[256,128]{0,1:T(8,128)}) %all-reduce.21.cloned.1.call-update) | async-done | bytes 131088 | tf_op jit(solution)/shard_map/psum | solution.py:131
  1070.4 1.9 convolution_convert_fusion.2
  1075.4 1.6 copy.44
  1077.7 22.2 %all_gather.7 = f32[256,128]{1,0:T(8,128)S(1)} all-gather(f32[16,128]{1,0:T(8,128)S(1)} %convolution_bitcast_fusion.21), channel_id=1, replica_groups=mesh['prow'=16,'pcol'=16] {'pcol'}, dimensions={0}, use_global_device_ids=true | all-gather | bytes 139264 | tf_op jit(solution)/shard_map/all_gather | solution.py:143
  1100.7 62.5 %all-reduce.23.cloned.1.call-done = f32[256,128]{0,1:T(8,128)} async-done(((f32[256,128]{0,1:T(8,128)}), f32[256,128]{0,1:T(8,128)}) %all-reduce.23.cloned.1.call-update) | async-done | bytes 131088 | tf_op jit(solution)/shard_map/psum | solution.py:143
  1164.4 1.3 fusion.130
  1166.4 1.7 convolution_add_fusion.1
  1171.9 2.0 fusion.121
  (269 shorter events, 42.9 us)
Async XLA Ops:
  7.2 26.6 %copy-start = (bf16[1,1,8,256,256]{4,3,2,1,0:T(8,128)(2,1)S(1)}, bf16[1,1,8,256,256]{4,3,2,1,0:T(8,128)(2,1)}, u32[]{:S(2)}) copy-start(bf16[1,1,8,256,256]{4,3,2,1,0:T(8,128)(2,1)} %param.54) | copy-start | bytes 3145732
  7.2 124.0 %all-reduce.9.cloned.1.call-start = ((), (), s32[]{:S(2)}) async-start(), calls=%async_computation | async-start | bytes 262144 | tf_op jit(solution)/shard_map/psum | solution.py:122
  10.6 20.6 %copy-start.79 = (bf16[7]{0:T(256)(128)(2,1)}, bf16[7]{0:T(256)(128)(2,1)S(1)}, u32[]{:S(2)}) copy-start(bf16[7]{0:T(256)(128)(2,1)S(1)} %fusion.590) | copy-start | bytes 46
  10.6 18.0 %copy-start.80 = (bf16[6]{0:T(256)(128)(2,1)}, bf16[6]{0:T(256)(128)(2,1)S(1)}, u32[]{:S(2)}) copy-start(bf16[6]{0:T(256)(128)(2,1)S(1)} %fusion.589) | copy-start | bytes 40
  10.6 14.7 %copy-start.81 = (bf16[5]{0:T(256)(128)(2,1)}, bf16[5]{0:T(256)(128)(2,1)S(1)}, u32[]{:S(2)}) copy-start(bf16[5]{0:T(256)(128)(2,1)S(1)} %fusion.588) | copy-start | bytes 34
  10.7 13.6 %copy-start.82 = (bf16[4]{0:T(256)(128)(2,1)}, bf16[4]{0:T(256)(128)(2,1)S(1)}, u32[]{:S(2)}) copy-start(bf16[4]{0:T(256)(128)(2,1)S(1)} %fusion.587) | copy-start | bytes 28
  10.7 13.6 %copy-start.83 = (bf16[3]{0:T(256)(128)(2,1)}, bf16[3]{0:T(256)(128)(2,1)S(1)}, u32[]{:S(2)}) copy-start(bf16[3]{0:T(256)(128)(2,1)S(1)} %fusion.586) | copy-start | bytes 22
  10.7 13.6 %copy-start.84 = (bf16[2]{0:T(256)(128)(2,1)}, bf16[2]{0:T(256)(128)(2,1)S(1)}, u32[]{:S(2)}) copy-start(bf16[2]{0:T(256)(128)(2,1)S(1)} %fusion.585) | copy-start | bytes 16
  12.1 12.2 %copy-start.45 = (f32[1,256]{1,0:T(1,128)}, f32[1,256]{1,0:T(1,128)S(1)}, u32[]{:S(2)}) copy-start(f32[1,256]{1,0:T(1,128)S(1)} %get-tuple-element.241) | copy-start | bytes 3076
  12.2 12.2 %copy-start.48 = (f32[1,256]{1,0:T(1,128)}, f32[1,256]{1,0:T(1,128)S(1)}, u32[]{:S(2)}) copy-start(f32[1,256]{1,0:T(1,128)S(1)} %get-tuple-element.240) | copy-start | bytes 3076
  12.2 12.2 %copy-start.61 = (f32[1,256]{1,0:T(1,128)}, f32[1,256]{1,0:T(1,128)S(1)}, u32[]{:S(2)}) copy-start(f32[1,256]{1,0:T(1,128)S(1)} %get-tuple-element.244) | copy-start | bytes 3076
  12.2 13.1 %copy-start.51 = (f32[1,256]{1,0:T(1,128)}, f32[1,256]{1,0:T(1,128)S(1)}, u32[]{:S(2)}) copy-start(f32[1,256]{1,0:T(1,128)S(1)} %get-tuple-element.239) | copy-start | bytes 3076
  12.2 16.4 %copy-start.54 = (f32[1,256]{1,0:T(1,128)}, f32[1,256]{1,0:T(1,128)S(1)}, u32[]{:S(2)}) copy-start(f32[1,256]{1,0:T(1,128)S(1)} %get-tuple-element.238) | copy-start | bytes 3076
  12.2 19.0 %copy-start.57 = (f32[1,256]{1,0:T(1,128)}, f32[1,256]{1,0:T(1,128)S(1)}, u32[]{:S(2)}) copy-start(f32[1,256]{1,0:T(1,128)S(1)} %get-tuple-element.237) | copy-start | bytes 3076
  15.9 11.8 %copy-start.26 = (bf16[128,256]{1,0:T(8,128)(2,1)}, bf16[128,256]{1,0:T(8,128)(2,1)S(1)}, u32[]{:S(2)}) copy-start(bf16[128,256]{1,0:T(8,128)(2,1)S(1)} %get-tuple-element.245) | copy-start | bytes 196612
  17.9 9.9 copy-start.28
  20.0 7.8 copy-start.31
  22.1 5.7 copy-start.34
  25.3 17.0 %copy-start.2 = (bf16[1,1,8,256,256]{4,3,2,1,0:T(8,128)(2,1)S(1)}, bf16[1,1,8,256,256]{4,3,2,1,0:T(8,128)(2,1)}, u32[]{:S(2)}) copy-start(bf16[1,1,8,256,256]{4,3,2,1,0:T(8,128)(2,1)} %param.56) | copy-start | bytes 3145732
  28.6 15.8 %copy-start.1 = (bf16[1,1,8,256,256]{4,3,2,1,0:T(8,128)(2,1)S(1)}, bf16[1,1,8,256,256]{4,3,2,1,0:T(8,128)(2,1)}, u32[]{:S(2)}) copy-start(bf16[1,1,8,256,256]{4,3,2,1,0:T(8,128)(2,1)} %param.55) | copy-start | bytes 3145732
  31.2 101.8 %copy-start.9 = (bf16[1,1,256,256]{3,2,1,0:T(8,128)(2,1)S(1)}, bf16[1,1,256,256]{3,2,1,0:T(8,128)(2,1)}, u32[]{:S(2)}) copy-start(bf16[1,1,256,256]{3,2,1,0:T(8,128)(2,1)} %param.57) | copy-start | bytes 393220
  33.8 101.0 %copy-start.25 = (bf16[1,16,256]{2,1,0:T(8,128)(2,1)S(1)}, bf16[1,16,256]{2,1,0:T(8,128)(2,1)}, u32[]{:S(2)}) copy-start(bf16[1,16,256]{2,1,0:T(8,128)(2,1)} %param.58) | copy-start | bytes 24580
  33.8 208.2 %copy-start.8 = (bf16[1,256,256]{2,1,0:T(8,128)(2,1)S(1)}, bf16[1,256,256]{2,1,0:T(8,128)(2,1)}, u32[]{:S(2)}) copy-start(bf16[1,256,256]{2,1,0:T(8,128)(2,1)} %param.51) | copy-start | bytes 393220
  33.8 456.7 %copy-start.10 = (bf16[256,256]{1,0:T(8,128)(2,1)S(1)}, bf16[256,256]{1,0:T(8,128)(2,1)}, u32[]{:S(2)}) copy-start(bf16[256,256]{1,0:T(8,128)(2,1)} %param.52) | copy-start | bytes 393220
  36.0 206.0 %all-reduce.11.cloned.1.call-start = ((), (), s32[]{:S(2)}) async-start(), calls=%async_computation.1 | async-start | bytes 262144 | tf_op jit(solution)/shard_map/psum | solution.py:127
  134.8 355.7 %all-reduce.13.cloned.1.call-start = ((), (), s32[]{:S(2)}) async-start(), calls=%async_computation.2 | async-start | bytes 262144 | tf_op jit(solution)/shard_map/psum | solution.py:131
  245.6 339.0 %all-reduce.15.cloned.1.call-start = ((), (), s32[]{:S(2)}) async-start(), calls=%async_computation.3 | async-start | bytes 262144 | tf_op jit(solution)/shard_map/psum | solution.py:143
  495.9 214.2 %all-reduce.17.cloned.1.call-start = ((), (), s32[]{:S(2)}) async-start(), calls=%async_computation.4 | async-start | bytes 262144 | tf_op jit(solution)/shard_map/psum | solution.py:122
  584.6 3.6 copy-start.12
  586.8 2.4 copy-start.3
  586.9 2.4 copy-start.70
  588.5 1.9 copy-start.38
  588.6 2.0 copy-start.68
  589.8 2.4 copy-start.32
  590.4 1.9 copy-start.72
  590.4 2.2 copy-start.29
  590.6 2.2 copy-start.19
  590.6 2.8 copy-start.27
  590.6 2.8 copy-start.62
  618.2 202.9 %all-reduce.19.cloned.1.call-start = ((), (), s32[]{:S(2)}) async-start(), calls=%async_computation.5 | async-start | bytes 262144 | tf_op jit(solution)/shard_map/psum | solution.py:127
  713.8 356.7 %all-reduce.21.cloned.1.call-start = ((), (), s32[]{:S(2)}) async-start(), calls=%async_computation.6 | async-start | bytes 262144 | tf_op jit(solution)/shard_map/psum | solution.py:131
  824.6 338.6 %all-reduce.23.cloned.1.call-start = ((), (), s32[]{:S(2)}) async-start(), calls=%async_computation.7 | async-start | bytes 262144 | tf_op jit(solution)/shard_map/psum | solution.py:143
  1073.5 94.6 %copy-start.11 = (bf16[128,256]{1,0:T(8,128)(2,1)S(1)}, bf16[128,256]{1,0:T(8,128)(2,1)}, u32[]{:S(2)}) copy-start(bf16[128,256]{1,0:T(8,128)(2,1)} %convolution_convert_fusion.2) | copy-start | bytes 196612
  1165.7 2.8 copy-start.44
  1165.7 2.8 copy-start.59
  1165.7 3.0 copy-start.71
  1166.4 2.1 copy-start.7
  1166.4 2.7 copy-start.4
  (45 other events, 60.7 us)
Sparse Core Ops, SparseCore 0:
  36.1 94.9 all-reduce.8
  134.9 107.0 all-reduce.10
  248.1 242.3 all-reduce.12
  496.0 88.5 all-reduce.14
  618.3 91.8 all-reduce.16
  713.9 107.1 all-reduce.18
  828.0 242.3 all-reduce.20
  1074.5 88.5 all-reduce.22
where the time goes:
time: 1180 us
  waiting for transfers between devices  999 us (85%)
  matrix products  92.7 us (8%)
  blocking collectives  46 us (4%)
  local copies, waits for them, and re-layouts  23.6 us (2%)
  between operations  16.2 us (1%)
    psum x2, waiting for transfers between devices, per_device(): lax.psum(summit_term + multiply(own_lift, own_strip, 'ki,kn->in'), ('prow...  489 us
    psum x2, waiting for transfers between devices, per_device(): strip_partial = lax.psum(strip_term, 'prow')  211 us
    psum x2, waiting for transfers between devices, per_device(): band_partial = lax.psum(band_term, 'pcol')  174 us
    psum x2, waiting for transfers between devices, per_device(): lax.psum(downward, 'pcol')  125 us
    dot_general x76, matrix products, multiply(): return jnp.einsum(form, left, right, preferred_element_type=jnp.float32)  92.7 us
    all_gather x2, blocking collectives, per_device(): lax.all_gather(band_piece, 'pcol', axis=0, tiled=True)  46 us
  transfers between devices with their start and end apart: 8, of which 8 were waited for; matrix products, arithmetic and copies ran while one was open for 2% of the time, Pallas kernels for 0%

commit v1 on v0

--- a/solution.py
+++ b/solution.py
@@ -129,7 +129,7 @@
         own_lift = lax.dynamic_slice_in_dim(lift_strip, row_place, strip_slab, 0)
         own_strip = lax.dynamic_slice_in_dim(strip_solved, row_place, strip_slab, 0)
         summit_partial = lax.psum(
-            summit_term + multiply(own_lift, own_strip, "ki,kn->in"), ("prow", "pcol")
+            lax.psum(summit_term + multiply(own_lift, own_strip, "ki,kn->in"), "pcol"), "prow"
         )
         summit_solved = forward_block(summit_inverse, summit_now, summit_partial)
         summit_answer = backward_block(

time: 1180 us -> 1110 us (0.941)
  waiting for transfers between devices: 999 us -> 918 us
    psum x2 -> x4, waiting for transfers between devices: 489 us -> 402 us  [the longest x2 218 us: per_device(): lax.psum(lax.psum(summit_term + multiply(own_lift, own_strip, 'ki,kn->in'...]
  transfers between devices with their start and end apart: 8 -> 10, of which waited for: 8 -> 10; matrix products, arithmetic and copies ran while one was open for 2% -> 2% of each run, Pallas kernels for 0% -> 0%
where the time goes in v1:
time: 1110 us; the launch traced here: 1100 us
  waiting for transfers between devices  918 us (83%)
  matrix products  92.7 us (8%)
  blocking collectives  48.6 us (4%)
  local copies, waits for them, and re-layouts  23.6 us (2%)
  between operations  16.2 us (1%)
    psum x2, waiting for transfers between devices, per_device(): lax.psum(lax.psum(summit_term + multiply(own_lift, own_strip, 'ki,kn->in'...  218 us
    psum x2, waiting for transfers between devices, per_device(): strip_partial = lax.psum(strip_term, 'prow')  211 us
    psum x2, waiting for transfers between devices, per_device(): lax.psum(summit_term + multiply(own_lift, own_strip, 'ki,kn->in'), 'pcol')  184 us
    psum x2, waiting for transfers between devices, per_device(): band_partial = lax.psum(band_term, 'pcol')  176 us
    psum x2, waiting for transfers between devices, per_device(): lax.psum(downward, 'pcol')  130 us
    dot_general x76, matrix products, multiply(): return jnp.einsum(form, left, right, preferred_element_type=jnp.float32)  92.7 us
    all_gather x2, blocking collectives, per_device(): lax.all_gather(band_piece, 'pcol', axis=0, tiled=True)  48.6 us
  transfers between devices with their start and end apart: 10, of which 10 were waited for; matrix products, arithmetic and copies ran while one was open for 2% of the time, Pallas kernels for 0%

profile of v1, /device:TPU:2, one launch (start us, length us, event | category | flops | bytes accessed | tf_op | source)
XLA Modules:
  0.0 1103.5 jit_solution(17837924078660387973)
XLA Ops:
  14.1 1.9 constant_dynamic-update-slice_fusion.17
  15.9 2.0 constant_dynamic-update-slice_fusion.16
  17.9 2.1 constant_dynamic-update-slice_fusion.15
  20.0 2.1 constant_dynamic-update-slice_fusion.14
  22.1 2.2 constant_dynamic-update-slice_fusion.13
  25.3 2.5 constant_dynamic-update-slice_fusion.12
  28.6 2.6 constant_dynamic-update-slice_fusion.11
  31.2 2.6 constant_dynamic-update-slice_fusion.18
  33.8 2.2 convolution_bitcast_fusion.19
  41.0 2.1 convolution_bitcast_fusion.17
  43.2 2.1 convolution_bitcast_fusion.18
  45.3 85.9 %all-reduce.11.cloned.1.call-done = f32[256,128]{1,0:T(8,128)} async-done(((f32[256,128]{1,0:T(8,128)}), f32[256,128]{1,0:T(8,128)}) %all-reduce.11.cloned.1.call-update) | async-done | bytes 131088 | tf_op jit(solution)/shard_map/psum | solution.py:122
  133.0 1.7 fusion.29
  134.8 1.8 fusion.34
  136.7 105.4 %all-reduce.13.cloned.1.call-done = f32[256,128]{1,0:T(8,128)} async-done(((f32[256,128]{1,0:T(8,128)}), f32[256,128]{1,0:T(8,128)}) %all-reduce.13.cloned.1.call-update) | async-done | bytes 131088 | tf_op jit(solution)/shard_map/psum | solution.py:127
  243.8 1.8 convolution_add_fusion.8
  246.8 91.5 %all-reduce.15.cloned.1.call-done = f32[256,128]{1,0:T(8,128)} async-done(((f32[256,128]{1,0:T(8,128)}), f32[256,128]{1,0:T(8,128)}) %all-reduce.15.cloned.1.call-update) | async-done | bytes 131088 | tf_op jit(solution)/shard_map/psum | solution.py:132
  339.6 108.2 %all-reduce.17.cloned.1.call-done = f32[256,128]{1,0:T(8,128)} async-done(((f32[256,128]{1,0:T(8,128)}), f32[256,128]{1,0:T(8,128)}) %all-reduce.17.cloned.1.call-update) | async-done | bytes 131088 | tf_op jit(solution)/shard_map/psum | solution.py:131
  447.7 1.9 convolution_convert_fusion.8
  449.6 1.9 convolution_convert_fusion.7
  451.5 1.7 convolution_bitcast_fusion.10
  454.2 25.1 %all_gather.6 = f32[256,128]{1,0:T(8,128)} all-gather(f32[16,128]{1,0:T(8,128)S(1)} %convolution_bitcast_fusion.22), channel_id=1, replica_groups=mesh['prow'=16,'pcol'=16] {'pcol'}, dimensions={0}, use_global_device_ids=true | all-gather | bytes 139264 | tf_op jit(solution)/shard_map/all_gather | solution.py:143
  479.3 1.6 copy.39
  481.0 64.8 %all-reduce.19.cloned.1.call-done = f32[256,128]{0,1:T(8,128)} async-done(((f32[256,128]{0,1:T(8,128)}), f32[256,128]{0,1:T(8,128)}) %all-reduce.19.cloned.1.call-update) | async-done | bytes 131088 | tf_op jit(solution)/shard_map/psum | solution.py:143
  556.1 2.0 constant_dynamic-update-slice_fusion.43
  558.1 2.1 constant_dynamic-update-slice_fusion.42
  560.2 2.2 constant_dynamic-update-slice_fusion.41
  562.4 2.4 constant_dynamic-update-slice_fusion.40
  564.8 2.4 constant_dynamic-update-slice_fusion.39
  567.2 2.5 constant_dynamic-update-slice_fusion.38
  569.7 2.6 constant_dynamic-update-slice_fusion.37
  572.3 2.7 constant_dynamic-update-slice_fusion.44
  575.0 2.2 convolution_bitcast_fusion.13
  577.2 2.2 convolution_bitcast_fusion.15
  579.4 2.2 convolution_bitcast_fusion.14
  581.6 89.7 %all-reduce.21.cloned.1.call-done = f32[256,128]{0,1:T(8,128)} async-done(((f32[256,128]{0,1:T(8,128)}), f32[256,128]{0,1:T(8,128)}) %all-reduce.21.cloned.1.call-update) | async-done | bytes 131088 | tf_op jit(solution)/shard_map/psum | solution.py:122
  673.1 1.8 fusion.27
  675.0 1.8 fusion.33
  676.8 105.4 %all-reduce.23.cloned.1.call-done = f32[256,128]{0,1:T(8,128)} async-done(((f32[256,128]{0,1:T(8,128)}), f32[256,128]{0,1:T(8,128)}) %all-reduce.23.cloned.1.call-update) | async-done | bytes 131088 | tf_op jit(solution)/shard_map/psum | solution.py:127
  783.9 1.8 convolution_add_fusion.6
  785.8 93.0 %all-reduce.25.cloned.1.call-done = f32[256,128]{0,1:T(8,128)} async-done(((f32[256,128]{0,1:T(8,128)}), f32[256,128]{0,1:T(8,128)}) %all-reduce.25.cloned.1.call-update) | async-done | bytes 131088 | tf_op jit(solution)/shard_map/psum | solution.py:132
  878.9 109.4 %all-reduce.27.cloned.1.call-done = f32[256,128]{0,1:T(8,128)} async-done(((f32[256,128]{0,1:T(8,128)}), f32[256,128]{0,1:T(8,128)}) %all-reduce.27.cloned.1.call-update) | async-done | bytes 131088 | tf_op jit(solution)/shard_map/psum | solution.py:131
  988.2 1.9 convolution_convert_fusion.2
  993.2 1.6 copy.44
  995.5 23.5 %all_gather.7 = f32[256,128]{1,0:T(8,128)S(1)} all-gather(f32[16,128]{1,0:T(8,128)S(1)} %convolution_bitcast_fusion.21), channel_id=1, replica_groups=mesh['prow'=16,'pcol'=16] {'pcol'}, dimensions={0}, use_global_device_ids=true | all-gather | bytes 139264 | tf_op jit(solution)/shard_map/all_gather | solution.py:143
  1019.8 65.1 %all-reduce.29.cloned.1.call-done = f32[256,128]{0,1:T(8,128)} async-done(((f32[256,128]{0,1:T(8,128)}), f32[256,128]{0,1:T(8,128)}) %all-reduce.29.cloned.1.call-update) | async-done | bytes 131088 | tf_op jit(solution)/shard_map/psum | solution.py:143
  1088.2 1.7 convolution_add_fusion.1
  1093.6 2.0 fusion.121
  (275 shorter events, 45.8 us)
Async XLA Ops:
  7.2 26.6 %copy-start = (bf16[1,1,8,256,256]{4,3,2,1,0:T(8,128)(2,1)S(1)}, bf16[1,1,8,256,256]{4,3,2,1,0:T(8,128)(2,1)}, u32[]{:S(2)}) copy-start(bf16[1,1,8,256,256]{4,3,2,1,0:T(8,128)(2,1)} %param.54) | copy-start | bytes 3145732
  7.2 124.0 %all-reduce.11.cloned.1.call-start = ((), (), s32[]{:S(2)}) async-start(), calls=%async_computation | async-start | bytes 262144 | tf_op jit(solution)/shard_map/psum | solution.py:122
  10.6 20.6 %copy-start.79 = (bf16[7]{0:T(256)(128)(2,1)}, bf16[7]{0:T(256)(128)(2,1)S(1)}, u32[]{:S(2)}) copy-start(bf16[7]{0:T(256)(128)(2,1)S(1)} %fusion.590) | copy-start | bytes 46
  10.6 18.0 %copy-start.80 = (bf16[6]{0:T(256)(128)(2,1)}, bf16[6]{0:T(256)(128)(2,1)S(1)}, u32[]{:S(2)}) copy-start(bf16[6]{0:T(256)(128)(2,1)S(1)} %fusion.589) | copy-start | bytes 40
  10.6 14.7 %copy-start.81 = (bf16[5]{0:T(256)(128)(2,1)}, bf16[5]{0:T(256)(128)(2,1)S(1)}, u32[]{:S(2)}) copy-start(bf16[5]{0:T(256)(128)(2,1)S(1)} %fusion.588) | copy-start | bytes 34
  10.7 13.6 %copy-start.82 = (bf16[4]{0:T(256)(128)(2,1)}, bf16[4]{0:T(256)(128)(2,1)S(1)}, u32[]{:S(2)}) copy-start(bf16[4]{0:T(256)(128)(2,1)S(1)} %fusion.587) | copy-start | bytes 28
  10.7 13.6 %copy-start.83 = (bf16[3]{0:T(256)(128)(2,1)}, bf16[3]{0:T(256)(128)(2,1)S(1)}, u32[]{:S(2)}) copy-start(bf16[3]{0:T(256)(128)(2,1)S(1)} %fusion.586) | copy-start | bytes 22
  10.7 13.6 %copy-start.84 = (bf16[2]{0:T(256)(128)(2,1)}, bf16[2]{0:T(256)(128)(2,1)S(1)}, u32[]{:S(2)}) copy-start(bf16[2]{0:T(256)(128)(2,1)S(1)} %fusion.585) | copy-start | bytes 16
  12.1 12.2 %copy-start.45 = (f32[1,256]{1,0:T(1,128)}, f32[1,256]{1,0:T(1,128)S(1)}, u32[]{:S(2)}) copy-start(f32[1,256]{1,0:T(1,128)S(1)} %get-tuple-element.241) | copy-start | bytes 3076
  12.2 12.2 %copy-start.48 = (f32[1,256]{1,0:T(1,128)}, f32[1,256]{1,0:T(1,128)S(1)}, u32[]{:S(2)}) copy-start(f32[1,256]{1,0:T(1,128)S(1)} %get-tuple-element.240) | copy-start | bytes 3076
  12.2 12.2 %copy-start.61 = (f32[1,256]{1,0:T(1,128)}, f32[1,256]{1,0:T(1,128)S(1)}, u32[]{:S(2)}) copy-start(f32[1,256]{1,0:T(1,128)S(1)} %get-tuple-element.244) | copy-start | bytes 3076
  12.2 13.1 %copy-start.51 = (f32[1,256]{1,0:T(1,128)}, f32[1,256]{1,0:T(1,128)S(1)}, u32[]{:S(2)}) copy-start(f32[1,256]{1,0:T(1,128)S(1)} %get-tuple-element.239) | copy-start | bytes 3076
  12.2 16.4 %copy-start.54 = (f32[1,256]{1,0:T(1,128)}, f32[1,256]{1,0:T(1,128)S(1)}, u32[]{:S(2)}) copy-start(f32[1,256]{1,0:T(1,128)S(1)} %get-tuple-element.238) | copy-start | bytes 3076
  12.2 19.0 %copy-start.57 = (f32[1,256]{1,0:T(1,128)}, f32[1,256]{1,0:T(1,128)S(1)}, u32[]{:S(2)}) copy-start(f32[1,256]{1,0:T(1,128)S(1)} %get-tuple-element.237) | copy-start | bytes 3076
  15.9 11.8 %copy-start.26 = (bf16[128,256]{1,0:T(8,128)(2,1)}, bf16[128,256]{1,0:T(8,128)(2,1)S(1)}, u32[]{:S(2)}) copy-start(bf16[128,256]{1,0:T(8,128)(2,1)S(1)} %get-tuple-element.245) | copy-start | bytes 196612
  17.9 9.9 copy-start.28
  20.0 7.8 copy-start.31
  22.1 5.7 copy-start.34
  25.3 15.7 %copy-start.2 = (bf16[1,1,8,256,256]{4,3,2,1,0:T(8,128)(2,1)S(1)}, bf16[1,1,8,256,256]{4,3,2,1,0:T(8,128)(2,1)}, u32[]{:S(2)}) copy-start(bf16[1,1,8,256,256]{4,3,2,1,0:T(8,128)(2,1)} %param.56) | copy-start | bytes 3145732
  28.6 14.6 %copy-start.1 = (bf16[1,1,8,256,256]{4,3,2,1,0:T(8,128)(2,1)S(1)}, bf16[1,1,8,256,256]{4,3,2,1,0:T(8,128)(2,1)}, u32[]{:S(2)}) copy-start(bf16[1,1,8,256,256]{4,3,2,1,0:T(8,128)(2,1)} %param.55) | copy-start | bytes 3145732
  31.2 101.8 %copy-start.9 = (bf16[1,1,256,256]{3,2,1,0:T(8,128)(2,1)S(1)}, bf16[1,1,256,256]{3,2,1,0:T(8,128)(2,1)}, u32[]{:S(2)}) copy-start(bf16[1,1,256,256]{3,2,1,0:T(8,128)(2,1)} %param.57) | copy-start | bytes 393220
  33.8 101.0 %copy-start.25 = (bf16[1,16,256]{2,1,0:T(8,128)(2,1)S(1)}, bf16[1,16,256]{2,1,0:T(8,128)(2,1)}, u32[]{:S(2)}) copy-start(bf16[1,16,256]{2,1,0:T(8,128)(2,1)} %param.58) | copy-start | bytes 24580
  33.8 208.2 %copy-start.8 = (bf16[1,256,256]{2,1,0:T(8,128)(2,1)S(1)}, bf16[1,256,256]{2,1,0:T(8,128)(2,1)}, u32[]{:S(2)}) copy-start(bf16[1,256,256]{2,1,0:T(8,128)(2,1)} %param.51) | copy-start | bytes 393220
  33.8 413.9 %copy-start.10 = (bf16[256,256]{1,0:T(8,128)(2,1)S(1)}, bf16[256,256]{1,0:T(8,128)(2,1)}, u32[]{:S(2)}) copy-start(bf16[256,256]{1,0:T(8,128)(2,1)} %param.52) | copy-start | bytes 393220
  36.0 206.0 %all-reduce.13.cloned.1.call-start = ((), (), s32[]{:S(2)}) async-start(), calls=%async_computation.1 | async-start | bytes 262144 | tf_op jit(solution)/shard_map/psum | solution.py:127
  134.8 203.6 %all-reduce.15.cloned.1.call-start = ((), (), s32[]{:S(2)}) async-start(), calls=%async_computation.2 | async-start | bytes 262144 | tf_op jit(solution)/shard_map/psum | solution.py:132
  245.6 202.1 %all-reduce.17.cloned.1.call-start = ((), (), s32[]{:S(2)}) async-start(), calls=%async_computation.3 | async-start | bytes 262144 | tf_op jit(solution)/shard_map/psum | solution.py:131
  338.3 207.5 %all-reduce.19.cloned.1.call-start = ((), (), s32[]{:S(2)}) async-start(), calls=%async_computation.4 | async-start | bytes 262144 | tf_op jit(solution)/shard_map/psum | solution.py:143
  453.1 218.1 %all-reduce.21.cloned.1.call-start = ((), (), s32[]{:S(2)}) async-start(), calls=%async_computation.5 | async-start | bytes 262144 | tf_op jit(solution)/shard_map/psum | solution.py:122
  545.8 3.6 copy-start.12
  548.0 2.4 copy-start.3
  548.0 2.4 copy-start.68
  549.7 2.0 copy-start.66
  551.0 2.4 copy-start.32
  551.6 2.2 copy-start.29
  551.8 2.2 copy-start.19
  551.8 2.8 copy-start.27
  551.8 2.8 copy-start.62
  579.3 202.8 %all-reduce.23.cloned.1.call-start = ((), (), s32[]{:S(2)}) async-start(), calls=%async_computation.6 | async-start | bytes 262144 | tf_op jit(solution)/shard_map/psum | solution.py:127
  674.9 203.9 %all-reduce.25.cloned.1.call-start = ((), (), s32[]{:S(2)}) async-start(), calls=%async_computation.7 | async-start | bytes 262144 | tf_op jit(solution)/shard_map/psum | solution.py:132
  785.7 202.5 %all-reduce.27.cloned.1.call-start = ((), (), s32[]{:S(2)}) async-start(), calls=%async_computation.8 | async-start | bytes 262144 | tf_op jit(solution)/shard_map/psum | solution.py:131
  878.8 206.1 %all-reduce.29.cloned.1.call-start = ((), (), s32[]{:S(2)}) async-start(), calls=%async_computation.9 | async-start | bytes 262144 | tf_op jit(solution)/shard_map/psum | solution.py:143
  991.4 98.5 %copy-start.11 = (bf16[128,256]{1,0:T(8,128)(2,1)S(1)}, bf16[128,256]{1,0:T(8,128)(2,1)}, u32[]{:S(2)}) copy-start(bf16[128,256]{1,0:T(8,128)(2,1)} %convolution_convert_fusion.2) | copy-start | bytes 196612
  1087.4 2.8 copy-start.44
  1087.4 2.8 copy-start.59
  1087.4 3.0 copy-start.69
  1088.2 2.1 copy-start.7
  1088.2 2.7 copy-start.4
  (47 other events, 64.5 us)
Sparse Core Ops, SparseCore 0:
  36.1 94.9 all-reduce.10
  134.9 107.0 all-reduce.12
  245.8 92.4 all-reduce.14
  340.6 107.0 all-reduce.16
  453.3 92.4 all-reduce.18
  579.5 91.7 all-reduce.20
  675.0 107.1 all-reduce.22
  786.3 92.4 all-reduce.24
  881.1 107.0 all-reduce.26
  992.3 92.4 all-reduce.28
